TPU v7x, 32 devices: a whole 2x2x4 slice. The times are simulated.
32 devices in a mesh: groups: 2 (over y), col: 4 (over x, core), row: 4 (over z).
Axes of the slice: x: 2, y: 2, z: 4, core: 2. Of those that a mesh axis runs over, the one named last changes fastest.
Arguments:
- features: bfloat16 [128, 128, 256], P(('groups', 'row'), 'col'), parts along dimension 0, may hold values from -6 to 6
- tissue: int32 [128, 128], P(('groups', 'row'), 'col'), parts along dimension 0, may hold values from 0 to 1, as said below
- conv_first: bfloat16 [3, 3, 256, 256], replicated, may hold values from -0.1875 to 0.1875
- bias_first: float32 [256], replicated, may hold values from -3 to 3
- conv_second: bfloat16 [3, 3, 256, 256], replicated, may hold values from -0.1875 to 0.1875
- bias_second: float32 [256], replicated, may hold values from -3 to 3
- key_weight: bfloat16 [256, 1280], replicated, may hold values from -0.375 to 0.375
- value_weight: bfloat16 [256, 1280], replicated, may hold values from -0.375 to 0.375
- latent_queries: bfloat16 [512, 1280], P(('col', 'row')), may hold values from -70 to 70
- out_weight: bfloat16 [1280, 1280], P(None, 'col'), may hold values from -0.15625 to 0.15625
Outputs:
- encoded: bfloat16 [1024, 1280], P(('groups', 'row'), 'col'), parts along dimension 0
There are 2 independent parts, one for each index of `groups`. A program takes and returns all parts, laid end to end along the dimension named above; an argument that names none is the same for every part. Nothing has to cross between parts.
Inputs may be any that keep to these rules, and one draw needn't show every extreme that they name: Every region of 16 x 32 patches of one device holds at least one tissue patch; the share of tissue differs widely from region to region.
All inputs are finite; a program needn't handle non-finite values.
Results may differ from a plain program's by a relative error of at most 0.007.
The roundings to bfloat16 on the way count: a program that leaves them out, or rounds other values in their place, can miss the bound.
Values may be sent and summed in bfloat16 or wider, within the bound.
A program may use at most 64 MiB of HBM per device.

v0:
```python
import math

import jax
import jax.numpy as jnp
from jax import lax
from jax.sharding import PartitionSpec as P


def padded_2(cells, sides, width):
    for axis, dim in sides:
        count = lax.axis_size(axis)
        ends = count - 1
        head = lax.slice_in_dim(cells, 0, width, axis=dim)
        tail = lax.slice_in_dim(cells, cells.shape[dim] - width, cells.shape[dim], axis=dim)
        cells = jnp.concatenate(
            [
                lax.ppermute(tail, axis, [(i, (i + 1) % count) for i in range(ends)]),
                cells,
                lax.ppermute(head, axis, [((i + 1) % count, i) for i in range(ends)]),
            ],
            axis=dim,
        )
    return cells


def convolve_valid(padded, weight, height, breadth):
    channels = padded.shape[2]
    summed = jnp.zeros((height * breadth, weight.shape[3]), jnp.float32)
    for offset_row in range(3):
        for offset_col in range(3):
            window = padded[offset_row : offset_row + height, offset_col : offset_col + breadth]
            summed = summed + jnp.dot(
                window.reshape(height * breadth, channels),
                weight[offset_row, offset_col],
                preferred_element_type=jnp.float32,
            )
    return summed.reshape(height, breadth, weight.shape[3])


def shards(
    features,
    tissue,
    conv_first,
    bias_first,
    conv_second,
    bias_second,
    key_weight,
    value_weight,
    latent_queries,
    out_weight,
):
    height, breadth, channels = features.shape
    keep_half = tissue.astype(jnp.bfloat16)
    keep_float = tissue.astype(jnp.float32)[:, :, None]
    inputs = features * keep_half[:, :, None]
    padded = padded_2(inputs, (("row", 0), ("col", 1)), 1)
    hidden = (
        jax.nn.gelu(
            convolve_valid(padded, conv_first, height, breadth) + bias_first, approximate=False
        )
        * keep_float
    ).astype(jnp.bfloat16)
    beside_all = padded_2(hidden, (("row", 0), ("col", 1)), 1)
    second = (
        jax.nn.gelu(
            convolve_valid(beside_all, conv_second, height, breadth) + bias_second,
            approximate=False,
        )
        * keep_float
    ).astype(jnp.bfloat16)
    flattened = second.reshape(height * breadth, channels)
    key_rows = jnp.dot(flattened, key_weight, preferred_element_type=jnp.float32).astype(
        jnp.bfloat16
    )
    queries = lax.all_gather(latent_queries, ("col", "row"), axis=0, tiled=True)
    latent_size = queries.shape[1]
    scale = 1.0 / math.sqrt(latent_size)
    scores = (
        lax.dot_general(
            queries, key_rows, (((1,), (1,)), ((), ())), preferred_element_type=jnp.float32
        )
        * scale
    )
    living = tissue.reshape(-1) > 0
    scores = jnp.where(living[None, :], scores, -1e30)
    local_top = jnp.max(scores, axis=1)
    top_score = lax.pmax(local_top, ("col", "row"))
    weights = jnp.exp(scores - top_score[:, None])
    denominator = jnp.sum(weights, axis=1)
    pooled = jnp.dot(weights.astype(jnp.bfloat16), flattened, preferred_element_type=jnp.float32)
    pooled_part, denom_part = (
        lax.psum_scatter(pooled, "row", scatter_dimension=0, tiled=True),
        lax.psum_scatter(denominator, "row", scatter_dimension=0, tiled=True),
    )
    pooled_whole, denom_whole = lax.psum((pooled_part, denom_part), "col")
    normalized = (pooled_whole / denom_whole[:, None]).astype(jnp.bfloat16)
    attended = jnp.dot(normalized, value_weight, preferred_element_type=jnp.float32).astype(
        jnp.bfloat16
    )
    return jnp.dot(attended, out_weight, preferred_element_type=jnp.float32).astype(jnp.bfloat16)


def solution(mesh):
    placed = (
        P(("groups", "row"), "col", None),
        P(("groups", "row"), "col"),
        P(),
        P(),
        P(),
        P(),
        P(),
        P(),
        P(("col", "row"), None),
        P(None, "col"),
    )
    return jax.shard_map(
        shards, mesh=mesh, in_specs=placed, out_specs=P(("groups", "row"), "col"), check_vma=False
    )
```

profile of v0, /device:TPU:0, one launch (start us, length us, event | category | flops | bytes accessed | tf_op | source)
XLA Modules:
  0.0 152.3 jit_solution(1866470164505878585)
XLA Ops:
  6.5 0.9 fusion.157
  7.4 1.1 broadcast_multiply_fusion
  8.5 4.9 %collective-permute-start = (bf16[1,32,256]{2,1,0:T(8,128)(2,1)S(1)}, bf16[1,32,256]{2,1,0:T(8,128)(2,1)S(1)}, u32[]{:S(2)}, u32[]{:S(2)}) collective-permute-start(bf16[1,32,256]{2,1,0:T(8,128)(2,1)S(1)} %get-tuple-element.31), channel_id=1, source_target_pairs={{0,1},{1,2},{2,3},{4,5},{5,6},{6,7},{8,9},{9,10},{10,11},{12,13},{... | collective-permute-start | bytes 49160 | tf_op jit(solution)/shard_map/ppermute | solution.py:17
  13.4 1.3 collective-permute-start.1
  14.9 4.2 %collective-permute-done.1 = bf16[1,32,256]{2,1,0:T(8,128)(2,1)S(1)} collective-permute-done((bf16[1,32,256]{2,1,0:T(8,128)(2,1)S(1)}, bf16[1,32,256]{2,1,0:T(8,128)(2,1)S(1)}, u32[]{:S(2)}, u32[]{:S(2)}) %collective-permute-start.1) | collective-permute-done | bytes 16416 | tf_op jit(solution)/shard_map/ppermute | solution.py:19
  19.1 1.3 collective-permute-start.2
  20.4 1.3 collective-permute-start.3
  21.8 0.2 fusion.98
  22.0 3.2 %collective-permute-done.3 = bf16[18,1,256]{2,1,0:T(2,128)(2,1)S(1)} collective-permute-done((bf16[18,1,256]{2,1,0:T(2,128)(2,1)S(1)}, bf16[18,1,256]{2,1,0:T(2,128)(2,1)S(1)}, u32[]{:S(2)}, u32[]{:S(2)}) %collective-permute-start.3) | collective-permute-done | bytes 9248 | tf_op jit(solution)/shard_map/ppermute | solution.py:19
  25.2 0.2 maximum_maximum_fusion
  25.6 0.2 fusion.90
  25.8 0.2 convolution_add_fusion.13
  26.1 0.2 convolution_add_fusion.12
  26.3 0.2 convolution_add_fusion.11
  26.5 0.2 convolution_add_fusion.10
  26.8 0.2 convolution_add_fusion.9
  27.0 0.2 convolution_add_fusion.8
  27.3 0.2 fusion.5
  27.5 0.4 copy-done.4
  27.9 1.2 fusion.13
  29.1 3.5 %collective-permute-start.4 = (bf16[1,32,256]{2,1,0:T(8,128)(2,1)S(1)}, bf16[1,32,256]{2,1,0:T(8,128)(2,1)S(1)}, u32[]{:S(2)}, u32[]{:S(2)}) collective-permute-start(bf16[1,32,256]{2,1,0:T(8,128)(2,1)S(1)} %get-tuple-element.27), channel_id=1, source_target_pairs={{0,1},{1,2},{2,3},{4,5},{5,6},{6,7},{8,9},{9,10},{10,11},{12,13},{... | collective-permute-start | bytes 49160 | tf_op jit(solution)/shard_map/ppermute | solution.py:17
  32.6 1.3 collective-permute-start.5
  34.1 4.1 %collective-permute-done.5 = bf16[1,32,256]{2,1,0:T(8,128)(2,1)S(1)} collective-permute-done((bf16[1,32,256]{2,1,0:T(8,128)(2,1)S(1)}, bf16[1,32,256]{2,1,0:T(8,128)(2,1)S(1)}, u32[]{:S(2)}, u32[]{:S(2)}) %collective-permute-start.5) | collective-permute-done | bytes 16416 | tf_op jit(solution)/shard_map/ppermute | solution.py:19
  38.3 3.4 %collective-permute-start.6 = (bf16[18,1,256]{2,1,0:T(2,128)(2,1)S(1)}, bf16[18,1,256]{2,1,0:T(2,128)(2,1)S(1)}, u32[]{:S(2)}, u32[]{:S(2)}) collective-permute-start(bf16[18,1,256]{2,1,0:T(2,128)(2,1)S(1)} %get-tuple-element.19), channel_id=1, source_target_pairs={{0,4},{4,8},{8,12},{1,5},{5,9},{9,13},{2,6},{6,10},{10,14},{3,7},{... | collective-permute-start | bytes 27656 | tf_op jit(solution)/shard_map/ppermute | solution.py:17
  41.7 1.3 collective-permute-start.7
  43.1 0.2 fusion.87
  43.3 2.0 %collective-permute-done.7 = bf16[18,1,256]{2,1,0:T(2,128)(2,1)S(1)} collective-permute-done((bf16[18,1,256]{2,1,0:T(2,128)(2,1)S(1)}, bf16[18,1,256]{2,1,0:T(2,128)(2,1)S(1)}, u32[]{:S(2)}, u32[]{:S(2)}) %collective-permute-start.7) | collective-permute-done | bytes 9248 | tf_op jit(solution)/shard_map/ppermute | solution.py:19
  45.3 0.2 maximum_maximum_fusion.1
  45.7 0.2 fusion.79
  46.0 0.2 convolution_add_fusion.6
  46.2 0.2 convolution_add_fusion.5
  46.4 0.2 convolution_add_fusion.4
  46.7 1.3 convolution_add_fusion.3
  48.0 0.2 convolution_add_fusion.2
  48.2 0.2 convolution_add_fusion.1
  48.4 0.2 copy-done.7
  48.7 1.4 fusion.21
  50.1 6.2 %all-gather.2.cloned.1.call-done = bf16[512,1280]{1,0:T(8,128)(2,1)} async-done(((bf16[32,1280]{1,0:T(8,128)(2,1)}), bf16[512,1280]{1,0:T(8,128)(2,1)}) %all-gather.2.cloned.1.call-update) | async-done | bytes 1310736 | tf_op jit(solution)/shard_map/all_gather | solution.py:75
  56.2 2.5 %fusion.158 = (f32[512]{0:T(512)S(1)}, f32[512,512]{1,0:T(8,128)S(1)}) fusion(bf16[512,1280]{1,0:T(8,128)(2,1)} %all-gather.2.cloned.1.call-done, bf16[512,256]{1,0:T(8,128)(2,1)S(1)} %fusion.21, bf16[256,1280]{1,0:T(8,128)(2,1)S(1)} %copy-done.5, pred[512]{0:T(512)(128)(4,1)S(1)} %gt.15), kind=kOutput, calls=%fused_computation.216 | convolution fusion | flops 1008074240 | bytes 3279360 | tf_op jit(solution)/shard_map/dot_general | solution.py:79
  58.8 31.5 %pmax.7 = f32[512]{0:T(512)S(1)} all-reduce(f32[512]{0:T(512)S(1)} %get-tuple-element.35), channel_id=1, replica_groups=mesh['groups'=2,'col'=4,'row'=4] {'col','row'}, use_global_device_ids=true, to_apply=%region_1.2 | all-reduce | flops 512 | bytes 4096 | tf_op jit(solution)/shard_map/pmax | solution.py:87
  90.3 1.2 fusion.22
  91.5 0.6 dynamic-slice
  92.8 18.8 %reduce-scatter.2.cloned.1.call-done = f32[128,256]{1,0:T(8,128)} async-done(((f32[512,256]{1,0:T(8,128)}), f32[128,256]{1,0:T(8,128)}) %reduce-scatter.2.cloned.1.call-update) | async-done | bytes 131088 | tf_op jit(solution)/shard_map/reduce_scatter | solution.py:92
  111.6 0.2 fusion.8
  111.8 8.7 %all-reduce = f32[512]{0:T(512)S(1)} all-reduce(f32[512]{0:T(512)S(1)} %fusion.8), channel_id=3, replica_groups=mesh['groups'=2,'col'=4,'row'=4] {'row'}, use_global_device_ids=true, to_apply=%region_5.6.clone | all-reduce | flops 512 | bytes 4096
  120.6 5.6 %psum.15 = f32[128]{0:T(128)S(1)} all-reduce(f32[128]{0:T(128)S(1)} %dynamic-slice.1), channel_id=1, replica_groups=mesh['groups'=2,'col'=4,'row'=4] {'col'}, use_global_device_ids=true, to_apply=%region_6.7 | all-reduce | flops 128 | bytes 1024 | tf_op jit(solution)/shard_map/psum | solution.py:95
  126.2 17.4 %all-reduce.3.cloned.1.call-done = f32[128,256]{1,0:T(8,128)} async-done(((f32[128,256]{1,0:T(8,128)}), f32[128,256]{1,0:T(8,128)}) %all-reduce.3.cloned.1.call-update) | async-done | bytes 131088 | tf_op jit(solution)/shard_map/psum | solution.py:95
  143.6 2.2 %fusion.7 = bf16[128,320]{0,1:T(8,128)(2,1)} fusion(bf16[1280,320]{0,1:T(8,128)(2,1)S(1)} %copy-done, bf16[256,1280]{1,0:T(8,128)(2,1)S(1)} %copy-done.6, f32[128,256]{1,0:T(8,128)} %all-reduce.3.cloned.1.call-done, f32[128]{0:T(128)S(1)} %psum.15), kind=kOutput, calls=%fused_computation.23 | convolution fusion | flops 189014016 | bytes 1688064 | tf_op jit(solution)/shard_map/dot_general | solution.py:100
  (39 shorter events, 1.0 us)
Async XLA Ops:
  6.5 137.1 %copy-start = (bf16[1280,320]{0,1:T(8,128)(2,1)S(1)}, bf16[1280,320]{0,1:T(8,128)(2,1)}, u32[]{:S(2)}) copy-start(bf16[1280,320]{0,1:T(8,128)(2,1)} %param.19) | copy-start | bytes 2457604
  6.5 15.2 %copy-start.1 = (bf16[3,3,256,256]{3,2,1,0:T(8,128)(2,1)S(1)}, bf16[3,3,256,256]{3,2,1,0:T(8,128)(2,1)}, u32[]{:S(2)}) copy-start(bf16[3,3,256,256]{3,2,1,0:T(8,128)(2,1)} %param.12) | copy-start | bytes 3538948
  6.5 49.7 %all-gather.2.cloned.1.call-start = ((), (), s32[]{:S(2)}) async-start(), calls=%async_computation.1 | async-start | bytes 1392640 | tf_op jit(solution)/shard_map/all_gather | solution.py:75
  8.5 6.4 %collective-permute-start = (bf16[1,32,256]{2,1,0:T(8,128)(2,1)S(1)}, bf16[1,32,256]{2,1,0:T(8,128)(2,1)S(1)}, u32[]{:S(2)}, u32[]{:S(2)}) collective-permute-start(bf16[1,32,256]{2,1,0:T(8,128)(2,1)S(1)} %get-tuple-element.31), channel_id=1, source_target_pairs={{0,1},{1,2},{2,3},{4,5},{5,6},{6,7},{8,9},{9,10},{10,11},{12,13},{... | collective-permute-start | bytes 49160 | tf_op jit(solution)/shard_map/ppermute | solution.py:17
  13.4 5.6 %collective-permute-start.1 = (bf16[1,32,256]{2,1,0:T(8,128)(2,1)S(1)}, bf16[1,32,256]{2,1,0:T(8,128)(2,1)S(1)}, u32[]{:S(2)}, u32[]{:S(2)}) collective-permute-start(bf16[1,32,256]{2,1,0:T(8,128)(2,1)S(1)} %get-tuple-element.32), channel_id=1, source_target_pairs={{1,0},{2,1},{3,2},{5,4},{6,5},{7,6},{9,8},{10,9},{11,10},{13,12},{... | collective-permute-start | bytes 49160 | tf_op jit(solution)/shard_map/ppermute | solution.py:19
  14.8 96.8 %reduce-scatter.2.cloned.1.call-start = ((), (), s32[]{:S(2)}) async-start(), calls=%async_computation.2 | async-start | bytes 655360 | tf_op jit(solution)/shard_map/reduce_scatter | solution.py:92
  19.1 2.9 %collective-permute-start.2 = (bf16[18,1,256]{2,1,0:T(2,128)(2,1)S(1)}, bf16[18,1,256]{2,1,0:T(2,128)(2,1)S(1)}, u32[]{:S(2)}, u32[]{:S(2)}) collective-permute-start(bf16[18,1,256]{2,1,0:T(2,128)(2,1)S(1)} %get-tuple-element.23), channel_id=1, source_target_pairs={{0,4},{4,8},{8,12},{1,5},{5,9},{9,13},{2,6},{6,10},{10,14},{3,7},{... | collective-permute-start | bytes 27656 | tf_op jit(solution)/shard_map/ppermute | solution.py:17
  20.4 4.8 %collective-permute-start.3 = (bf16[18,1,256]{2,1,0:T(2,128)(2,1)S(1)}, bf16[18,1,256]{2,1,0:T(2,128)(2,1)S(1)}, u32[]{:S(2)}, u32[]{:S(2)}) collective-permute-start(bf16[18,1,256]{2,1,0:T(2,128)(2,1)S(1)} %get-tuple-element.24), channel_id=1, source_target_pairs={{4,0},{8,4},{12,8},{5,1},{9,5},{13,9},{6,2},{10,6},{14,10},{7,3},{... | collective-permute-start | bytes 27656 | tf_op jit(solution)/shard_map/ppermute | solution.py:19
  27.2 0.7 copy-start.4
  27.2 6.7 %copy-start.3 = (s32[16,32]{1,0:T(8,128)S(1)}, s32[16,32]{1,0:T(8,128)}, u32[]{:S(2)}) copy-start(s32[16,32]{1,0:T(8,128)} %param.11) | copy-start | bytes 6148
  27.5 15.6 %copy-start.2 = (bf16[3,3,256,256]{3,2,1,0:T(8,128)(2,1)S(1)}, bf16[3,3,256,256]{3,2,1,0:T(8,128)(2,1)}, u32[]{:S(2)}) copy-start(bf16[3,3,256,256]{3,2,1,0:T(8,128)(2,1)} %param.14) | copy-start | bytes 3538948
  29.1 5.0 %collective-permute-start.4 = (bf16[1,32,256]{2,1,0:T(8,128)(2,1)S(1)}, bf16[1,32,256]{2,1,0:T(8,128)(2,1)S(1)}, u32[]{:S(2)}, u32[]{:S(2)}) collective-permute-start(bf16[1,32,256]{2,1,0:T(8,128)(2,1)S(1)} %get-tuple-element.27), channel_id=1, source_target_pairs={{0,1},{1,2},{2,3},{4,5},{5,6},{6,7},{8,9},{9,10},{10,11},{12,13},{... | collective-permute-start | bytes 49160 | tf_op jit(solution)/shard_map/ppermute | solution.py:17
  32.6 5.6 %collective-permute-start.5 = (bf16[1,32,256]{2,1,0:T(8,128)(2,1)S(1)}, bf16[1,32,256]{2,1,0:T(8,128)(2,1)S(1)}, u32[]{:S(2)}, u32[]{:S(2)}) collective-permute-start(bf16[1,32,256]{2,1,0:T(8,128)(2,1)S(1)} %get-tuple-element.28), channel_id=1, source_target_pairs={{1,0},{2,1},{3,2},{5,4},{6,5},{7,6},{9,8},{10,9},{11,10},{13,12},{... | collective-permute-start | bytes 49160 | tf_op jit(solution)/shard_map/ppermute | solution.py:19
  38.3 5.0 %collective-permute-start.6 = (bf16[18,1,256]{2,1,0:T(2,128)(2,1)S(1)}, bf16[18,1,256]{2,1,0:T(2,128)(2,1)S(1)}, u32[]{:S(2)}, u32[]{:S(2)}) collective-permute-start(bf16[18,1,256]{2,1,0:T(2,128)(2,1)S(1)} %get-tuple-element.19), channel_id=1, source_target_pairs={{0,4},{4,8},{8,12},{1,5},{5,9},{9,13},{2,6},{6,10},{10,14},{3,7},{... | collective-permute-start | bytes 27656 | tf_op jit(solution)/shard_map/ppermute | solution.py:17
  41.7 3.6 %collective-permute-start.7 = (bf16[18,1,256]{2,1,0:T(2,128)(2,1)S(1)}, bf16[18,1,256]{2,1,0:T(2,128)(2,1)S(1)}, u32[]{:S(2)}, u32[]{:S(2)}) collective-permute-start(bf16[18,1,256]{2,1,0:T(2,128)(2,1)S(1)} %get-tuple-element.20), channel_id=1, source_target_pairs={{4,0},{8,4},{12,8},{5,1},{9,5},{13,9},{6,2},{10,6},{14,10},{7,3},{... | collective-permute-start | bytes 27656 | tf_op jit(solution)/shard_map/ppermute | solution.py:19
  48.0 0.7 copy-start.7
  48.7 7.6 %copy-start.5 = (bf16[256,1280]{1,0:T(8,128)(2,1)S(1)}, bf16[256,1280]{1,0:T(8,128)(2,1)}, u32[]{:S(2)}) copy-start(bf16[256,1280]{1,0:T(8,128)(2,1)} %param.16) | copy-start | bytes 1966084
  90.3 1.2 copy-start.8
  91.5 52.1 %copy-start.6 = (bf16[256,1280]{1,0:T(8,128)(2,1)S(1)}, bf16[256,1280]{1,0:T(8,128)(2,1)}, u32[]{:S(2)}) copy-start(bf16[256,1280]{1,0:T(8,128)(2,1)} %param.17) | copy-start | bytes 1966084
  91.5 52.1 %all-reduce.3.cloned.1.call-start = ((), (), s32[]{:S(2)}) async-start(), calls=%async_computation.3 | async-start | bytes 262144 | tf_op jit(solution)/shard_map/psum | solution.py:95
Sparse Core Ops, SparseCore 0:
  14.9 41.3 all-gather.1
  91.6 19.9 reduce-scatter.1
  113.9 29.6 all-reduce.2
where the time goes:
time: 153 us; the launch traced here: 152 us
  waiting for transfers between devices  56 us (37%)
  blocking collectives  45.9 us (30%)
  starting transfers between devices  18.4 us (12%)
  between operations  14.1 us (9%)
  matrix products  12.2 us (8%)
  other arithmetic  3.89 us (3%)
  local copies, waits for them, and re-layouts  1.87 us (1%)
    pmax x1, blocking collectives, shards(): top_score = lax.pmax(local_top, ('col', 'row'))  31.5 us
    reduce_scatter x1, waiting for transfers between devices, shards(): lax.psum_scatter(pooled, 'row', scatter_dimension=0, tiled=True)  18.8 us
    psum x1, waiting for transfers between devices, shards(): pooled_whole, denom_whole = lax.psum((pooled_part, denom_part), 'col')  17.4 us
    ppermute x4, waiting for transfers between devices, padded_2(): lax.ppermute(head, axis, [((i + 1) % count, i) for i in range(ends)])  13.5 us
    ppermute x4, starting transfers between devices, padded_2(): lax.ppermute(tail, axis, [(i, (i + 1) % count) for i in range(ends)])  13.1 us
    unnamed x1, blocking collectives  8.71 us
    dot_general x18, matrix products, convolve_valid(): jnp.dot(window.reshape(height * breadth, channels), weight[offset_row, of...  6.34 us
    all_gather x1, waiting for transfers between devices, shards(): queries = lax.all_gather(latent_queries, ('col', 'row'), axis=0, tiled=True)  6.18 us
  transfers between devices with their start and end apart: 11, of which 8 were waited for; matrix products, arithmetic and copies ran while one was open for 6% of the time, Pallas kernels for 0%

commit v1 on v0

--- a/solution.py
+++ b/solution.py
@@ -1,9 +1,419 @@
+import functools
 import math
 
 import jax
 import jax.numpy as jnp
 from jax import lax
+from jax.experimental import pallas as pl
+from jax.experimental.pallas import tpu as pltpu
 from jax.sharding import PartitionSpec as P
+
+MESH = pl.DeviceIdType.MESH
+LANES = 128
+EDGE = 16
+DIRS = ((-1, 0), (1, 0), (0, -1), (0, 1), (-1, -1), (-1, 1), (1, -1), (1, 1))
+
+
+def divisor(total, largest):
+    return max(d for d in range(1, largest + 1) if total % d == 0)
+
+
+def gelu(x):
+    return 0.5 * x * (1.0 + lax.erf(x * math.sqrt(0.5)))
+
+
+def kernel(
+    nrow, ncol,
+    feat, tis, w1, b1, w2, b2, kw, vw, lq, ow,
+    out,
+    feat_v, tis_v, w1_v, b1_v, w2_v, b2_v, kw_v, vw_v, ow_v,
+    cells, packed, col_out, corner_out, row_in, col_in, corner_in,
+    shifted1, hidden, shifted2, second_t, keys, queries,
+    pool_out, stat_out, pool_in, stat_in, norm_all,
+    load_sem, halo_send, halo_recv, qz_send, qz_recv, qx_send, qx_recv, qp_send, qp_recv,
+    pool_send, pool_recv, stat_send, stat_recv, norm_send, norm_recv,
+):
+    height, breadth, channels = feat.shape
+    own, latent = lq.shape
+    per_row = own * nrow
+    share = channels // ncol
+    nx = ncol // 2
+    row, col = lax.axis_index("row"), lax.axis_index("col")
+    x, core = col // 2, col % 2
+    me = row * ncol + col
+    reach = breadth + 2 * EDGE
+    wide = breadth + EDGE
+
+    loads = [
+        pltpu.make_async_copy(src, dst, load_sem.at[i])
+        for i, (src, dst) in enumerate(
+            [
+                (feat, feat_v), (tis, tis_v), (w1, w1_v), (b1, b1_v), (w2, w2_v), (b2, b2_v),
+                (kw, kw_v), (vw, vw_v), (ow, ow_v),
+                (lq, queries.at[pl.ds(pl.multiple_of((col * nrow + row) * own, own), own)]),
+            ]
+        )
+    ]
+    barrier = pltpu.get_barrier_semaphore()
+    loads[1].start()
+    loads[0].start()
+    for step in range(1, nrow * ncol):
+        other = lax.rem(me + step, nrow * ncol)
+        pl.semaphore_signal(
+            barrier, inc=1, device_id={"row": other // ncol, "col": other % ncol},
+            device_id_type=MESH,
+        )
+    for i in (9, 2, 3, 4, 5, 6, 7, 8):
+        loads[i].start()
+
+    loads[1].wait()
+    mask = jnp.broadcast_to(tis_v[...].astype(jnp.float32)[:, :, None], (height, breadth, LANES))
+    loads[0].wait()
+    cells[2 : 2 + height, EDGE : EDGE + breadth, channels:] = mask
+    packed[:, :, channels:] = mask.astype(jnp.bfloat16)
+    for part in range(0, channels, LANES):
+        kept = feat_v[:, :, part : part + LANES].astype(jnp.float32) * mask
+        cells[2 : 2 + height, EDGE : EDGE + breadth, part : part + LANES] = kept
+        packed[:, :, part : part + LANES] = kept.astype(jnp.bfloat16)
+    for side, first in enumerate((0, breadth - 2)):
+        for ci in range(2):
+            col_out[side, ci] = cells[2 : 2 + height, EDGE + first + ci, :].astype(jnp.bfloat16)
+    for k, (dr, dc) in enumerate(DIRS[4:]):
+        r0 = 2 if dr < 0 else height
+        c0 = EDGE if dc < 0 else EDGE + breadth - 2
+        rows = [cells[r0 + i, c0 + j : c0 + j + 1, :] for i in range(2) for j in range(2)]
+        corner_out[k] = jnp.concatenate(
+            rows + [jnp.zeros((EDGE - 4, rows[0].shape[1]), jnp.float32)], axis=0
+        ).astype(jnp.bfloat16)
+
+    pl.semaphore_wait(barrier, nrow * ncol - 1)
+
+    def inside(r, c):
+        return jnp.logical_and(
+            jnp.logical_and(r >= 0, r < nrow), jnp.logical_and(c >= 0, c < ncol)
+        )
+
+    def halo_copy(d):
+        dr, dc = DIRS[d]
+        if d < 2:
+            src = packed.at[0:2] if dr < 0 else packed.at[height - 2 : height]
+            dst = row_in.at[d]
+        elif d < 4:
+            src, dst = col_out.at[d - 2], col_in.at[d - 2]
+        else:
+            src, dst = corner_out.at[d - 4], corner_in.at[d - 4]
+        return pltpu.make_async_remote_copy(
+            src_ref=src, dst_ref=dst, send_sem=halo_send.at[d], recv_sem=halo_recv.at[d],
+            device_id={
+                "row": lax.rem(row + dr + nrow, nrow), "col": lax.rem(col + dc + ncol, ncol)
+            },
+            device_id_type=MESH,
+        )
+
+    for d, (dr, dc) in enumerate(DIRS):
+        @pl.when(inside(row + dr, col + dc))
+        def _():
+            halo_copy(d).start()
+
+    def block(c, r):
+        return pl.ds(pl.multiple_of((c * nrow + r) * own, own), own)
+
+    def chunk(c):
+        return pl.ds(pl.multiple_of(c * per_row, per_row), per_row)
+
+    def z_copy(step, wait=False):
+        target = lax.rem(row + step, nrow)
+        owner = lax.rem(row - step + nrow, nrow) if wait else row
+        return pltpu.make_async_remote_copy(
+            src_ref=lq, dst_ref=queries.at[block(col, owner)],
+            send_sem=qz_send.at[step], recv_sem=qz_recv.at[step],
+            device_id={"row": target}, device_id_type=MESH,
+        )
+
+    def x_copy(t, step, wait=False):
+        owner = lax.rem(row - step + nrow, nrow)
+        source = 2 * lax.rem(x - t + nx, nx) + core if wait else col
+        return pltpu.make_async_remote_copy(
+            src_ref=lq if step == 0 else queries.at[block(col, owner)],
+            dst_ref=queries.at[block(source, owner)],
+            send_sem=qx_send.at[t, step], recv_sem=qx_recv.at[t, step],
+            device_id={"col": 2 * lax.rem(x + t, nx) + core}, device_id_type=MESH,
+        )
+
+    def pair_copy(t, wait=False):
+        origin = 2 * lax.rem(x - t + nx, nx) + (1 - core if wait else core)
+        return pltpu.make_async_remote_copy(
+            src_ref=queries.at[chunk(origin)], dst_ref=queries.at[chunk(origin)],
+            send_sem=qp_send.at[t], recv_sem=qp_recv.at[t],
+            device_id={"col": 2 * x + 1 - core}, device_id_type=MESH,
+        )
+
+    for step in range(1, nrow):
+        z_copy(step).start()
+    for t in range(1, nx):
+        x_copy(t, 0).start()
+
+    for d, (dr, dc) in enumerate(DIRS):
+        there = inside(row - dr, col - dc)
+        r0 = (2 + height if dr < 0 else 0) if dr else 2
+        c0 = (EDGE + breadth if dc < 0 else EDGE - 2) if dc else EDGE
+
+        @pl.when(there)
+        def _():
+            halo_copy(d).wait_recv()
+            if d < 2:
+                cells[r0 : r0 + 2, EDGE : EDGE + breadth, :] = row_in[d].astype(jnp.float32)
+            elif d < 4:
+                for ci in range(2):
+                    cells[2 : 2 + height, c0 + ci, :] = col_in[d - 2, ci].astype(jnp.float32)
+            else:
+                got = corner_in[d - 4].astype(jnp.float32)
+                for i in range(2):
+                    for j in range(2):
+                        cells[r0 + i, c0 + j : c0 + j + 1, :] = got[2 * i + j : 2 * i + j + 1]
+
+        @pl.when(jnp.logical_not(there))
+        def _():
+            rows = 2 if dr else height
+            cols = 2 if dc else breadth
+            cells[r0 : r0 + rows, c0 : c0 + cols, :] = jnp.zeros(
+                (rows, cols, cells.shape[2]), jnp.float32
+            )
+
+    half = EDGE // 2
+    for b in range(3):
+        shifted1[b] = cells[:, half - 1 + b : half - 1 + b + wide, :channels].astype(jnp.bfloat16)
+
+    loads[2].wait()
+    loads[3].wait()
+    rows1 = divisor(height + 2, 6)
+
+    @pl.loop(0, (height + 2) // rows1)
+    def _(i):
+        top = i * rows1
+        lhs = jnp.concatenate(
+            [
+                shifted1[b, pl.ds(top + a, rows1)].reshape(rows1 * wide, channels)
+                for a in range(3)
+                for b in range(3)
+            ],
+            axis=1,
+        )
+        acc = jnp.dot(lhs, w1_v[...], preferred_element_type=jnp.float32)
+        acted = gelu(acc + b1_v[...]).reshape(rows1, wide, channels)
+        keep = cells[pl.ds(top + 1, rows1), half : half + wide, channels:]
+        for part in range(0, channels, LANES):
+            hidden[pl.ds(top, rows1), :, part : part + LANES] = (
+                acted[:, :, part : part + LANES] * keep
+            )
+
+    for step in range(1, nrow):
+        z_copy(step, True).wait_recv()
+        for t in range(1, nx):
+            x_copy(t, step).start()
+    loads[9].wait()
+    pair_copy(0).start()
+
+    for b in range(3):
+        shifted2[b] = hidden[:, half - 1 + b : half - 1 + b + breadth, :].astype(jnp.bfloat16)
+    loads[4].wait()
+    loads[5].wait()
+    loads[6].wait()
+    rows2 = divisor(height, 4)
+    span = rows2 * breadth
+    keep_all = cells[2 : 2 + height, EDGE : EDGE + breadth, channels:].reshape(-1, LANES)
+
+    for i in range(height // rows2):
+        top = i * rows2
+        lhs = jnp.concatenate(
+            [
+                shifted2[b, top + a : top + a + rows2].reshape(span, channels)
+                for a in range(3)
+                for b in range(3)
+            ],
+            axis=1,
+        )
+        acc = jnp.dot(lhs, w2_v[...], preferred_element_type=jnp.float32)
+        acted = gelu(acc + b2_v[...])
+        keep = keep_all[i * span : (i + 1) * span]
+        second = jnp.concatenate(
+            [acted[:, part : part + LANES] * keep for part in range(0, channels, LANES)], axis=1
+        )
+        second_t[:, i * span : (i + 1) * span] = second.T.astype(jnp.bfloat16)
+        keys[i * span : (i + 1) * span] = jnp.dot(
+            second.astype(jnp.bfloat16), kw_v[...], preferred_element_type=jnp.float32
+        ).astype(jnp.bfloat16)
+
+    scale = 1.0 / math.sqrt(latent)
+    pair_copy(0, True).wait_recv()
+
+    def pool_copy(r, c, source):
+        return pltpu.make_async_remote_copy(
+            src_ref=pool_out.at[r, pl.ds(pl.multiple_of(c * share, share), share)],
+            dst_ref=pool_in.at[source],
+            send_sem=pool_send.at[r * ncol + c], recv_sem=pool_recv.at[source],
+            device_id={"row": r, "col": c}, device_id_type=MESH,
+        )
+
+    def stat_copy(r, c, source):
+        return pltpu.make_async_remote_copy(
+            src_ref=stat_out.at[r], dst_ref=stat_in.at[source],
+            send_sem=stat_send.at[r * ncol + c], recv_sem=stat_recv.at[source],
+            device_id={"row": r, "col": c}, device_id_type=MESH,
+        )
+
+    for t in range(nx):
+        if t:
+            for step in range(nrow):
+                x_copy(t, step, True).wait_recv()
+            pair_copy(t).start()
+            pair_copy(t, True).wait_recv()
+        kx = lax.rem(x - t + nx, nx)
+        got = queries[pl.ds(pl.multiple_of(kx * 2 * per_row, 2 * per_row), 2 * per_row), :]
+        scores = (
+            lax.dot_general(
+                keys[...], got, (((1,), (1,)), ((), ())), preferred_element_type=jnp.float32
+            )
+            * scale
+        )
+        living = jnp.concatenate([keep_all] * (2 * per_row // LANES), axis=1) > 0
+        scores = jnp.where(living, scores, -1e30)
+        top_score = jnp.max(scores, axis=0, keepdims=True)
+        weights = jnp.exp(scores - top_score)
+        denominator = jnp.sum(weights, axis=0, keepdims=True)
+        pooled = jnp.dot(
+            second_t[...], weights.astype(jnp.bfloat16), preferred_element_type=jnp.float32
+        ).astype(jnp.bfloat16)
+        for side in range(2):
+            r = 2 * kx + side
+            cut = slice(side * per_row, (side + 1) * per_row)
+            pool_out[r] = pooled[:, cut]
+            stat_out[r, 0:1] = top_score[:, cut]
+            stat_out[r, 1:2] = denominator[:, cut]
+            for c in range(ncol):
+                mine = jnp.logical_and(r == row, c == col)
+
+                @pl.when(jnp.logical_not(mine))
+                def _():
+                    stat_copy(r, c, me).start()
+                    pool_copy(r, c, me).start()
+
+    pool_in[me] = pool_out[row, pl.ds(pl.multiple_of(col * share, share), share), :]
+    stat_in[me] = stat_out[row]
+
+    for step in range(1, nrow * ncol):
+        source = lax.rem(me + step, nrow * ncol)
+        stat_copy(0, 0, source).wait_recv()
+    tops = stat_in[:, 0, :]
+    best = jnp.max(tops, axis=0, keepdims=True)
+    factors = jnp.exp(tops - best)
+    denom = jnp.sum(factors * stat_in[:, 1, :], axis=0, keepdims=True)
+    for step in range(1, nrow * ncol):
+        source = lax.rem(me + step, nrow * ncol)
+        pool_copy(0, 0, source).wait_recv()
+    total = jnp.zeros((share, per_row), jnp.float32)
+    for s in range(nrow * ncol):
+        total = total + pool_in[s].astype(jnp.float32) * factors[s : s + 1]
+    my_share = pl.ds(pl.multiple_of(col * share, share), share)
+    norm_all[my_share, :] = (total / denom).astype(jnp.bfloat16)
+
+    def norm_copy(step, wait=False):
+        owner = lax.rem(col - step + ncol, ncol) if wait else col
+        place = pl.ds(pl.multiple_of(owner * share, share), share)
+        return pltpu.make_async_remote_copy(
+            src_ref=norm_all.at[place], dst_ref=norm_all.at[place],
+            send_sem=norm_send.at[step], recv_sem=norm_recv.at[step],
+            device_id={"col": lax.rem(col + step, ncol)}, device_id_type=MESH,
+        )
+
+    for step in range(1, ncol):
+        norm_copy(step).start()
+    loads[7].wait()
+    loads[8].wait()
+    for step in range(1, ncol):
+        norm_copy(step, True).wait_recv()
+    normalized = norm_all[...].astype(jnp.float32).T.astype(jnp.bfloat16)
+    attended = jnp.dot(normalized, vw_v[...], preferred_element_type=jnp.float32).astype(
+        jnp.bfloat16
+    )
+    out[...] = jnp.dot(attended, ow_v[...], preferred_element_type=jnp.float32).astype(out.dtype)
+
+    for d, (dr, dc) in enumerate(DIRS):
+        @pl.when(inside(row + dr, col + dc))
+        def _():
+            halo_copy(d).wait_send()
+    for step in range(1, nrow):
+        z_copy(step).wait_send()
+    for t in range(1, nx):
+        for step in range(nrow):
+            x_copy(t, step).wait_send()
+    for t in range(nx):
+        pair_copy(t).wait_send()
+    for step in range(1, nrow * ncol):
+        other = lax.rem(me + step, nrow * ncol)
+        stat_copy(other // ncol, other % ncol, me).wait_send()
+        pool_copy(other // ncol, other % ncol, me).wait_send()
+    for step in range(1, ncol):
+        norm_copy(step).wait_send()
+
+
+def in_one(nrow, ncol, features, tissue, conv_first, bias_first, conv_second, bias_second,
+           key_weight, value_weight, latent_queries, out_weight):
+    height, breadth, channels = features.shape
+    own, latent = latent_queries.shape
+    total = own * nrow * ncol
+    per_row = total // nrow
+    share = channels // ncol
+    nx = ncol // 2
+    everyone = nrow * ncol
+    columns = out_weight.shape[1]
+    depth = channels + LANES
+    reach = breadth + 2 * EDGE
+    wide = breadth + EDGE
+    half, full = jnp.bfloat16, jnp.float32
+    w1 = conv_first.reshape(-1, conv_first.shape[3])
+    w2 = conv_second.reshape(-1, conv_second.shape[3])
+    b1 = bias_first.reshape(1, -1)
+    b2 = bias_second.reshape(1, -1)
+    operands = (features, tissue, w1, b1, w2, b2, key_weight, value_weight, latent_queries,
+                out_weight)
+    held = [operands[i] for i in (0, 1, 2, 3, 4, 5, 6, 7, 9)]
+    dma = pltpu.SemaphoreType.DMA
+    return pl.pallas_call(
+        functools.partial(kernel, nrow, ncol),
+        out_shape=jax.ShapeDtypeStruct((per_row, columns), half),
+        in_specs=[pl.BlockSpec(memory_space=pl.ANY)] * len(operands),
+        out_specs=pl.BlockSpec(memory_space=pltpu.VMEM),
+        scratch_shapes=[pltpu.VMEM(a.shape, a.dtype) for a in held]
+        + [
+            pltpu.VMEM((height + 4, reach, depth), full),
+            pltpu.VMEM((height, breadth, depth), half),
+            pltpu.VMEM((2, 2, height, depth), half),
+            pltpu.VMEM((4, EDGE, depth), half),
+            pltpu.VMEM((2, 2, breadth, depth), half),
+            pltpu.VMEM((2, 2, height, depth), half),
+            pltpu.VMEM((4, EDGE, depth), half),
+            pltpu.VMEM((3, height + 4, wide, channels), half),
+            pltpu.VMEM((height + 2, wide, channels), full),
+            pltpu.VMEM((3, height + 2, breadth, channels), half),
+            pltpu.VMEM((channels, height * breadth), half),
+            pltpu.VMEM((height * breadth, latent), half),
+            pltpu.VMEM((total, latent), half),
+            pltpu.VMEM((nrow, channels, per_row), half),
+            pltpu.VMEM((nrow, 8, per_row), full),
+            pltpu.VMEM((everyone, share, per_row), half),
+            pltpu.VMEM((everyone, 8, per_row), full),
+            pltpu.VMEM((channels, per_row), half),
+            dma((10,)), dma((8,)), dma((8,)), dma((nrow,)), dma((nrow,)),
+            dma((nx, nrow)), dma((nx, nrow)), dma((nx,)), dma((nx,)),
+            dma((everyone,)), dma((everyone,)), dma((everyone,)), dma((everyone,)),
+            dma((ncol,)), dma((ncol,)),
+        ],
+        compiler_params=pltpu.CompilerParams(
+            collective_id=0, has_side_effects=True, vmem_limit_bytes=50 * 1024 * 1024
+        ),
+        cost_estimate=pl.CostEstimate(flops=2_500_000_000, bytes_accessed=8_000_000, transcendentals=0),
+    )(*operands)
 
 
 def padded_2(cells, sides, width):
@@ -100,7 +510,24 @@
     return jnp.dot(attended, out_weight, preferred_element_type=jnp.float32).astype(jnp.bfloat16)
 
 
+def fits(nrow, ncol, arrays):
+    height, breadth, channels = arrays[0].shape
+    own, latent = arrays[8].shape
+    return (
+        nrow == ncol
+        and ncol % 2 == 0
+        and own % 16 == 0
+        and (own * ncol) % LANES == 0
+        and (channels // ncol) % 16 == 0
+        and channels % LANES == 0
+        and height % 16 == 0
+        and breadth % 16 == 0
+        and latent % LANES == 0
+    )
+
+
 def solution(mesh):
+    nrow, ncol = mesh.shape["row"], mesh.shape["col"]
     placed = (
         P(("groups", "row"), "col", None),
         P(("groups", "row"), "col"),
@@ -113,6 +540,12 @@
         P(("col", "row"), None),
         P(None, "col"),
     )
+
+    def either(*arrays):
+        if fits(nrow, ncol, arrays):
+            return in_one(nrow, ncol, *arrays)
+        return shards(*arrays)
+
     return jax.shard_map(
-        shards, mesh=mesh, in_specs=placed, out_specs=P(("groups", "row"), "col"), check_vma=False
-    )
+        either, mesh=mesh, in_specs=placed, out_specs=P(("groups", "row"), "col"), check_vma=False
+    )

time: 153 us -> 38.5 us (0.25)
  waiting for transfers between devices: 56 us -> 0 us
  blocking collectives: 45.9 us -> 0 us
  Pallas kernels: 0 us -> 33.2 us
  starting transfers between devices: 18.4 us -> 0 us
  between operations: 14.1 us -> 0.09 us
  matrix products: 12.2 us -> 0 us
  other arithmetic: 3.89 us -> 0 us
  local copies, waits for them, and re-layouts: 1.87 us -> 4.61 us
    pallas_call x0 -> x1, Pallas kernels: none -> 33.2 us  [in_one(): pl.pallas_call(functools.partial(kernel, nrow, ncol), out_shape=jax.Shape...]
    pmax x1 -> x0, blocking collectives: 31.5 us -> none  [shards(): top_score = lax.pmax(local_top, ('col', 'row'))]
    reduce_scatter x1 -> x0, waiting for transfers between devices: 18.8 us -> none  [shards(): lax.psum_scatter(pooled, 'row', scatter_dimension=0, tiled=True)]
    ppermute x8 -> x0, starting transfers between devices: 18.3 us -> none  [the longest x4 13.1 us: padded_2(): lax.ppermute(tail, axis, [(i, (i + 1) % count) for i in range(ends)])]
    psum x1 -> x0, waiting for transfers between devices: 17.4 us -> none  [shards(): pooled_whole, denom_whole = lax.psum((pooled_part, denom_part), 'col')]
    ppermute x8 -> x0, waiting for transfers between devices: 13.6 us -> none  [the longest x4 13.5 us: padded_2(): lax.ppermute(head, axis, [((i + 1) % count, i) for i in range(ends)])]
    dot_general x21 -> x0, matrix products: 12.2 us -> none  [the longest x18 6.34 us: convolve_valid(): jnp.dot(window.reshape(height * breadth, channels), weight[offset_row, of...]
    unnamed x1 -> x0, blocking collectives: 8.71 us -> none
  transfers between devices with their start and end apart: 11 -> 0, of which waited for: 8 -> 0; matrix products, arithmetic and copies ran while one was open for 6% -> 0% of each run, Pallas kernels for 0% -> 0%
where the time goes in v1:
time: 38.5 us; the launch traced here: 37.9 us
  Pallas kernels  33.2 us (86%)
  local copies, waits for them, and re-layouts  4.61 us (12%)
    pallas_call x1, Pallas kernels, in_one(): pl.pallas_call(functools.partial(kernel, nrow, ncol), out_shape=jax.Shape...  33.2 us
    unnamed x17, local copies, waits for them, and re-layouts  3.86 us

profile of v1, /device:TPU:0, one launch (start us, length us, event | category | flops | bytes accessed | tf_op | source)
XLA Modules:
  0.0 37.9 jit_solution(6794089415914795507)
XLA Ops:
  0.0 0.0 copy-start.4
  0.0 0.0 copy-start.7
  0.0 0.0 copy-start.6
  0.0 0.0 copy-start
  0.0 0.0 copy-start.5
  0.0 0.0 copy-start.3
  0.0 1.7 %copy.11.ow = bf16[1280,320]{1,0:T(8,128)(2,1)S(1)} copy(bf16[1280,320]{0,1:T(8,128)(2,1)} %param.19) | data formatting | bytes 1638400 | tf_op args[9]
  1.7 0.0 copy-done.4
  1.7 0.0 copy-done.7
  1.7 0.0 copy-done.6
  1.7 0.0 copy-done
  1.7 0.0 copy-done.5
  1.7 0.0 copy-done.3
  1.8 0.0 copy-start.1
  1.8 1.1 %copy-done.1 = bf16[256,1280]{1,0:T(8,128)(2,1)S(1)} copy-done((bf16[256,1280]{1,0:T(8,128)(2,1)S(1)}, bf16[256,1280]{1,0:T(8,128)(2,1)}, u32[]{:S(2)}) %copy-start.1) | copy-done | bytes 655384
  2.9 0.0 copy-start.2
  2.9 1.1 %copy-done.2 = bf16[256,1280]{1,0:T(8,128)(2,1)S(1)} copy-done((bf16[256,1280]{1,0:T(8,128)(2,1)S(1)}, bf16[256,1280]{1,0:T(8,128)(2,1)}, u32[]{:S(2)}) %copy-start.2) | copy-done | bytes 655384
  3.9 33.2 %shard_map.100 = bf16[128,320]{1,0:T(8,128)(2,1)S(1)} custom-call(bf16[16,32,256]{2,1,0:T(8,128)(2,1)S(1)} %copy-done.3, s32[16,32]{1,0:T(8,128)S(1)} %copy-done.5, bf16[2304,256]{1,0:T(8,128)(2,1)S(1)} %bitcast.4, f32[1,256]{1,0:T(1,128)S(1)} %bitcast.5, bf16[2304,256]{1,0:T(8,128)(2,1)} %bitcast.7, f32[1,256]{1,0:T(1,128)S(1)} %bitcast.6, ...), custom_call_target="tpu_custom_call" | custom-call | flops 2500000000 | bytes 8000000 | tf_op jit(solution)/shard_map/pallas_call | solution.py:382
  37.1 0.7 %copy.12 = bf16[128,320]{0,1:T(8,128)(2,1)} copy(bf16[128,320]{1,0:T(8,128)(2,1)S(1)} %shard_map.100) | data formatting | bytes 163840 | tf_op jit(solution)/shard_map/pallas_call | solution.py:382
Async XLA Ops:
  0.0 1.7 %copy-start.4 = (bf16[32,1280]{1,0:T(8,128)(2,1)S(1)}, bf16[32,1280]{1,0:T(8,128)(2,1)}, u32[]{:S(2)}) copy-start(bf16[32,1280]{1,0:T(8,128)(2,1)} %lq.1) | copy-start | bytes 245764
  0.0 1.7 %copy-start.7 = (f32[256]{0:T(256)S(1)}, f32[256]{0:T(256)}, u32[]{:S(2)}) copy-start(f32[256]{0:T(256)} %param.15) | copy-start | bytes 3076
  0.0 1.7 %copy-start.6 = (f32[256]{0:T(256)S(1)}, f32[256]{0:T(256)}, u32[]{:S(2)}) copy-start(f32[256]{0:T(256)} %param.13) | copy-start | bytes 3076
  0.0 1.7 %copy-start = (bf16[3,3,256,256]{3,2,1,0:T(8,128)(2,1)S(1)}, bf16[3,3,256,256]{3,2,1,0:T(8,128)(2,1)}, u32[]{:S(2)}) copy-start(bf16[3,3,256,256]{3,2,1,0:T(8,128)(2,1)} %param.12) | copy-start | bytes 3538948
  0.0 1.7 %copy-start.5 = (s32[16,32]{1,0:T(8,128)S(1)}, s32[16,32]{1,0:T(8,128)}, u32[]{:S(2)}) copy-start(s32[16,32]{1,0:T(8,128)} %tis.1) | copy-start | bytes 6148
  0.0 1.7 %copy-start.3 = (bf16[16,32,256]{2,1,0:T(8,128)(2,1)S(1)}, bf16[16,32,256]{2,1,0:T(8,128)(2,1)}, u32[]{:S(2)}) copy-start(bf16[16,32,256]{2,1,0:T(8,128)(2,1)} %feat.1) | copy-start | bytes 786436
  1.8 1.1 %copy-start.1 = (bf16[256,1280]{1,0:T(8,128)(2,1)S(1)}, bf16[256,1280]{1,0:T(8,128)(2,1)}, u32[]{:S(2)}) copy-start(bf16[256,1280]{1,0:T(8,128)(2,1)} %kw.1) | copy-start | bytes 1966084
  2.9 1.1 %copy-start.2 = (bf16[256,1280]{1,0:T(8,128)(2,1)S(1)}, bf16[256,1280]{1,0:T(8,128)(2,1)}, u32[]{:S(2)}) copy-start(bf16[256,1280]{1,0:T(8,128)(2,1)} %vw.1) | copy-start | bytes 1966084

commit v2 on v1

--- a/solution.py
+++ b/solution.py
@@ -28,9 +28,9 @@
     out,
     feat_v, tis_v, w1_v, b1_v, w2_v, b2_v, kw_v, vw_v, ow_v,
     cells, packed, col_out, corner_out, row_in, col_in, corner_in,
-    shifted1, hidden, shifted2, second_t, keys, queries,
+    shifted1, hidden, shifted2, second_own, second_in, keep_in, second_t, keys, queries,
     pool_out, stat_out, pool_in, stat_in, norm_all,
-    load_sem, halo_send, halo_recv, qz_send, qz_recv, qx_send, qx_recv, qp_send, qp_recv,
+    load_sem, halo_send, halo_recv, qz_send, qz_recv, qx_send, qx_recv, pair_send, pair_recv,
     pool_send, pool_recv, stat_send, stat_recv, norm_send, norm_recv,
 ):
     height, breadth, channels = feat.shape
@@ -41,7 +41,11 @@
     row, col = lax.axis_index("row"), lax.axis_index("col")
     x, core = col // 2, col % 2
     me = row * ncol + col
-    reach = breadth + 2 * EDGE
+    me_chip = row * nx + x
+    rows2 = divisor(height, 4)
+    span = rows2 * breadth
+    spans = height // rows2
+    count = height * breadth
     wide = breadth + EDGE
 
     loads = [
@@ -140,14 +144,18 @@
             device_id={"col": 2 * lax.rem(x + t, nx) + core}, device_id_type=MESH,
         )
 
-    def pair_copy(t, wait=False):
-        origin = 2 * lax.rem(x - t + nx, nx) + (1 - core if wait else core)
-        return pltpu.make_async_remote_copy(
-            src_ref=queries.at[chunk(origin)], dst_ref=queries.at[chunk(origin)],
-            send_sem=qp_send.at[t], recv_sem=qp_recv.at[t],
+    def pair_copy(i):
+        if i < spans:
+            src = second_own.at[i * span : (i + 1) * span]
+            dst = second_in.at[i * span : (i + 1) * span]
+        else:
+            src, dst = packed.at[:, :, channels:], keep_in
+        return pltpu.make_async_remote_copy(
+            src_ref=src, dst_ref=dst, send_sem=pair_send.at[i], recv_sem=pair_recv.at[i],
             device_id={"col": 2 * x + 1 - core}, device_id_type=MESH,
         )
 
+    pair_copy(spans).start()
     for step in range(1, nrow):
         z_copy(step).start()
     for t in range(1, nx):
@@ -207,23 +215,19 @@
                 acted[:, :, part : part + LANES] * keep
             )
 
-    for step in range(1, nrow):
+    def hand_on(step):
         z_copy(step, True).wait_recv()
         for t in range(1, nx):
             x_copy(t, step).start()
-    loads[9].wait()
-    pair_copy(0).start()
 
     for b in range(3):
         shifted2[b] = hidden[:, half - 1 + b : half - 1 + b + breadth, :].astype(jnp.bfloat16)
     loads[4].wait()
     loads[5].wait()
     loads[6].wait()
-    rows2 = divisor(height, 4)
-    span = rows2 * breadth
     keep_all = cells[2 : 2 + height, EDGE : EDGE + breadth, channels:].reshape(-1, LANES)
 
-    for i in range(height // rows2):
+    for i in range(spans):
         top = i * rows2
         lhs = jnp.concatenate(
             [
@@ -239,13 +243,37 @@
         second = jnp.concatenate(
             [acted[:, part : part + LANES] * keep for part in range(0, channels, LANES)], axis=1
         )
+        second_half = second.astype(jnp.bfloat16)
+        second_own[i * span : (i + 1) * span] = second_half
+        pair_copy(i).start()
         second_t[:, i * span : (i + 1) * span] = second.T.astype(jnp.bfloat16)
         keys[i * span : (i + 1) * span] = jnp.dot(
-            second.astype(jnp.bfloat16), kw_v[...], preferred_element_type=jnp.float32
+            second_half, kw_v[...], preferred_element_type=jnp.float32
         ).astype(jnp.bfloat16)
+        if i + 1 < nrow:
+            hand_on(i + 1)
+    for step in range(spans + 1, nrow):
+        hand_on(step)
+
+    for i in range(spans):
+        pair_copy(i).wait_recv()
+        second_half = second_in[i * span : (i + 1) * span]
+        place = slice(count + i * span, count + (i + 1) * span)
+        second_t[:, place] = second_half.astype(jnp.float32).T.astype(jnp.bfloat16)
+        keys[place] = jnp.dot(
+            second_half, kw_v[...], preferred_element_type=jnp.float32
+        ).astype(jnp.bfloat16)
+    pair_copy(spans).wait_recv()
+    living = (
+        jnp.concatenate(
+            [keep_all, keep_in[...].astype(jnp.float32).reshape(-1, LANES)], axis=0
+        )
+        > 0
+    )
+    living = jnp.concatenate([living] * (per_row // LANES), axis=1)
 
     scale = 1.0 / math.sqrt(latent)
-    pair_copy(0, True).wait_recv()
+    loads[9].wait()
 
     def pool_copy(r, c, source):
         return pltpu.make_async_remote_copy(
@@ -266,17 +294,14 @@
         if t:
             for step in range(nrow):
                 x_copy(t, step, True).wait_recv()
-            pair_copy(t).start()
-            pair_copy(t, True).wait_recv()
-        kx = lax.rem(x - t + nx, nx)
-        got = queries[pl.ds(pl.multiple_of(kx * 2 * per_row, 2 * per_row), 2 * per_row), :]
+        r = 2 * lax.rem(x - t + nx, nx) + core
+        got = queries[chunk(r), :]
         scores = (
             lax.dot_general(
                 keys[...], got, (((1,), (1,)), ((), ())), preferred_element_type=jnp.float32
             )
             * scale
         )
-        living = jnp.concatenate([keep_all] * (2 * per_row // LANES), axis=1) > 0
         scores = jnp.where(living, scores, -1e30)
         top_score = jnp.max(scores, axis=0, keepdims=True)
         weights = jnp.exp(scores - top_score)
@@ -284,35 +309,36 @@
         pooled = jnp.dot(
             second_t[...], weights.astype(jnp.bfloat16), preferred_element_type=jnp.float32
         ).astype(jnp.bfloat16)
-        for side in range(2):
-            r = 2 * kx + side
-            cut = slice(side * per_row, (side + 1) * per_row)
-            pool_out[r] = pooled[:, cut]
-            stat_out[r, 0:1] = top_score[:, cut]
-            stat_out[r, 1:2] = denominator[:, cut]
-            for c in range(ncol):
-                mine = jnp.logical_and(r == row, c == col)
-
-                @pl.when(jnp.logical_not(mine))
-                def _():
-                    stat_copy(r, c, me).start()
-                    pool_copy(r, c, me).start()
-
-    pool_in[me] = pool_out[row, pl.ds(pl.multiple_of(col * share, share), share), :]
-    stat_in[me] = stat_out[row]
-
-    for step in range(1, nrow * ncol):
-        source = lax.rem(me + step, nrow * ncol)
-        stat_copy(0, 0, source).wait_recv()
+        pool_out[r] = pooled
+        stat_out[r, 0:1] = top_score
+        stat_out[r, 1:2] = denominator
+        for c in range(ncol):
+            @pl.when(jnp.logical_not(jnp.logical_and(r == row, c == col)))
+            def _():
+                stat_copy(r, c, me_chip).start()
+                pool_copy(r, c, me_chip).start()
+
+    own_part = core == row % 2
+
+    @pl.when(own_part)
+    def _():
+        pool_in[me_chip] = pool_out[row, pl.ds(pl.multiple_of(col * share, share), share), :]
+        stat_in[me_chip] = stat_out[row]
+
+    def from_all(copy):
+        for source in range(nrow * nx):
+            @pl.when(jnp.logical_not(jnp.logical_and(own_part, source == me_chip)))
+            def _():
+                copy(0, 0, source).wait_recv()
+
+    from_all(stat_copy)
     tops = stat_in[:, 0, :]
     best = jnp.max(tops, axis=0, keepdims=True)
     factors = jnp.exp(tops - best)
     denom = jnp.sum(factors * stat_in[:, 1, :], axis=0, keepdims=True)
-    for step in range(1, nrow * ncol):
-        source = lax.rem(me + step, nrow * ncol)
-        pool_copy(0, 0, source).wait_recv()
+    from_all(pool_copy)
     total = jnp.zeros((share, per_row), jnp.float32)
-    for s in range(nrow * ncol):
+    for s in range(nrow * nx):
         total = total + pool_in[s].astype(jnp.float32) * factors[s : s + 1]
     my_share = pl.ds(pl.multiple_of(col * share, share), share)
     norm_all[my_share, :] = (total / denom).astype(jnp.bfloat16)
@@ -336,7 +362,9 @@
     attended = jnp.dot(normalized, vw_v[...], preferred_element_type=jnp.float32).astype(
         jnp.bfloat16
     )
-    out[...] = jnp.dot(attended, ow_v[...], preferred_element_type=jnp.float32).astype(out.dtype)
+    out[...] = lax.dot_general(
+        ow_v[...], attended, (((1,), (1,)), ((), ())), preferred_element_type=jnp.float32
+    ).astype(out.dtype)
 
     for d, (dr, dc) in enumerate(DIRS):
         @pl.when(inside(row + dr, col + dc))
@@ -347,12 +375,15 @@
     for t in range(1, nx):
         for step in range(nrow):
             x_copy(t, step).wait_send()
+    for i in range(spans + 1):
+        pair_copy(i).wait_send()
     for t in range(nx):
-        pair_copy(t).wait_send()
-    for step in range(1, nrow * ncol):
-        other = lax.rem(me + step, nrow * ncol)
-        stat_copy(other // ncol, other % ncol, me).wait_send()
-        pool_copy(other // ncol, other % ncol, me).wait_send()
+        r = 2 * lax.rem(x - t + nx, nx) + core
+        for c in range(ncol):
+            @pl.when(jnp.logical_not(jnp.logical_and(r == row, c == col)))
+            def _():
+                stat_copy(r, c, me_chip).wait_send()
+                pool_copy(r, c, me_chip).wait_send()
     for step in range(1, ncol):
         norm_copy(step).wait_send()
 
@@ -366,6 +397,8 @@
     share = channels // ncol
     nx = ncol // 2
     everyone = nrow * ncol
+    sources = nrow * nx
+    spans = height // divisor(height, 4) + 1
     columns = out_weight.shape[1]
     depth = channels + LANES
     reach = breadth + 2 * EDGE
@@ -376,13 +409,13 @@
     b1 = bias_first.reshape(1, -1)
     b2 = bias_second.reshape(1, -1)
     operands = (features, tissue, w1, b1, w2, b2, key_weight, value_weight, latent_queries,
-                out_weight)
+                out_weight.T)
     held = [operands[i] for i in (0, 1, 2, 3, 4, 5, 6, 7, 9)]
     dma = pltpu.SemaphoreType.DMA
     return pl.pallas_call(
         functools.partial(kernel, nrow, ncol),
-        out_shape=jax.ShapeDtypeStruct((per_row, columns), half),
-        in_specs=[pl.BlockSpec(memory_space=pl.ANY)] * len(operands),
+        out_shape=jax.ShapeDtypeStruct((columns, per_row), half),
+        in_specs=[pl.BlockSpec(memory_space=pltpu.HBM)] * len(operands),
         out_specs=pl.BlockSpec(memory_space=pltpu.VMEM),
         scratch_shapes=[pltpu.VMEM(a.shape, a.dtype) for a in held]
         + [
@@ -396,24 +429,27 @@
             pltpu.VMEM((3, height + 4, wide, channels), half),
             pltpu.VMEM((height + 2, wide, channels), full),
             pltpu.VMEM((3, height + 2, breadth, channels), half),
-            pltpu.VMEM((channels, height * breadth), half),
-            pltpu.VMEM((height * breadth, latent), half),
+            pltpu.VMEM((height * breadth, channels), half),
+            pltpu.VMEM((height * breadth, channels), half),
+            pltpu.VMEM((height, breadth, LANES), half),
+            pltpu.VMEM((channels, 2 * height * breadth), half),
+            pltpu.VMEM((2 * height * breadth, latent), half),
             pltpu.VMEM((total, latent), half),
             pltpu.VMEM((nrow, channels, per_row), half),
             pltpu.VMEM((nrow, 8, per_row), full),
-            pltpu.VMEM((everyone, share, per_row), half),
-            pltpu.VMEM((everyone, 8, per_row), full),
+            pltpu.VMEM((sources, share, per_row), half),
+            pltpu.VMEM((sources, 8, per_row), full),
             pltpu.VMEM((channels, per_row), half),
             dma((10,)), dma((8,)), dma((8,)), dma((nrow,)), dma((nrow,)),
-            dma((nx, nrow)), dma((nx, nrow)), dma((nx,)), dma((nx,)),
-            dma((everyone,)), dma((everyone,)), dma((everyone,)), dma((everyone,)),
+            dma((nx, nrow)), dma((nx, nrow)), dma((spans,)), dma((spans,)),
+            dma((everyone,)), dma((sources,)), dma((everyone,)), dma((sources,)),
             dma((ncol,)), dma((ncol,)),
         ],
         compiler_params=pltpu.CompilerParams(
-            collective_id=0, has_side_effects=True, vmem_limit_bytes=50 * 1024 * 1024
+            collective_id=0, has_side_effects=True, vmem_limit_bytes=63 * 1024 * 1024
         ),
         cost_estimate=pl.CostEstimate(flops=2_500_000_000, bytes_accessed=8_000_000, transcendentals=0),
-    )(*operands)
+    )(*operands).T
 
 
 def padded_2(cells, sides, width):

time: 38.5 us -> 34.5 us (0.90); the launches traced: 37.9 us -> 34.3 us
  local copies, waits for them, and re-layouts: 4.61 us -> 1.53 us
  Pallas kernels: 33.2 us -> 32.7 us
    unnamed x17 -> x1, local copies, waits for them, and re-layouts: 3.86 us -> 1.53 us
    pallas_call x1 -> x0, local copies, waits for them, and re-layouts: 0.75 us -> none  [in_one(): pl.pallas_call(functools.partial(kernel, nrow, ncol), out_shape=jax.Shape...]
    pallas_call x1, Pallas kernels: 33.2 us -> 32.7 us  [in_one(): pl.pallas_call(functools.partial(kernel, nrow, ncol), out_shape=jax.Shape...]
where the time goes in v2:
time: 34.5 us; the launch traced here: 34.3 us
  Pallas kernels  32.7 us (95%)
  local copies, waits for them, and re-layouts  1.53 us (4%)
    pallas_call x1, Pallas kernels, in_one(): pl.pallas_call(functools.partial(kernel, nrow, ncol), out_shape=jax.Shape...  32.7 us
    unnamed x1, local copies, waits for them, and re-layouts  1.53 us

profile of v2, /device:TPU:0, one launch (start us, length us, event | category | flops | bytes accessed | tf_op | source)
XLA Modules:
  0.0 34.3 jit_solution(17511411105484144310)
XLA Ops:
  0.0 32.7 %shard_map.100 = bf16[320,128]{1,0:T(8,128)(2,1)} custom-call(bf16[16,32,256]{2,1,0:T(8,128)(2,1)} %feat.1, s32[16,32]{1,0:T(8,128)} %tis.1, bf16[2304,256]{1,0:T(8,128)(2,1)} %bitcast.7, f32[1,256]{1,0:T(1,128)} %bitcast.10, bf16[2304,256]{1,0:T(8,128)(2,1)} %bitcast.8, f32[1,256]{1,0:T(1,128)} %bitcast.11, bf16[256,1280]{1,0:T(8,128)(2,1)} %kw.1, ...), custom_call_target="tpu_custom_call" | custom-call | flops 2500000000 | bytes 8000000 | tf_op jit(solution)/shard_map/pallas_call | solution.py:415
  32.8 1.5 %copy.12 = bf16[128,320]{0,1:T(8,128)(2,1)} copy(bf16[128,320]{0,1:T(8,128)(2,1)} %bitcast.6) | data formatting | bytes 163840
